TPU v7x, 256 devices: a whole 4x4x8 slice. The times are simulated.
256 devices in a mesh: cell: 32 (over z_lo, y, core), gene: 8 (over z_hi, x).
Axes of the slice: x: 4, y: 4, z: 8 (z_hi: 2, z_lo: 4; z = z_hi * 4 + z_lo), core: 2. Of those that a mesh axis runs over, the one named last changes fastest.
Arguments:
- counts: bfloat16 [65536, 16384], P('cell', 'gene'), may hold values from 0 to 25, as said below
- cell_factor: float32 [32, 65536], P(None, 'cell'), may hold values from 0.15 to 4.5, as said below
- gene_factor: float32 [32, 16384], P(None, 'gene'), may hold values from 0.15 to 4.5, as said below
Outputs:
- cell_result: float32 [32, 65536], P(None, 'cell')
- gene_result: float32 [32, 16384], P(None, 'gene')
Inputs may be any that keep to these rules, and one draw needn't show every extreme that they name: `counts`: whole numbers. `cell_factor`: positive. `gene_factor`: positive.
All inputs are finite; a program needn't handle non-finite values.
Results may differ from a plain program's by a relative error of at most 0.001.
Values sent between devices are 32-bit elements; how exact they have to be, the bound alone decides.
No kernel may reach another device: no remote copies, remote signals or barrier semaphores. Data moves between devices by JAX's collectives and lax.ppermute only.
A program may use at most 64 MiB of HBM per device.

v0:
```python
import jax
import jax.numpy as jnp
from jax import lax
from jax.sharding import PartitionSpec as P

ITERS = 3


def ratio_tile(counts, cell_copy, gene_copy):
    approx = lax.dot_general(
        cell_copy, gene_copy, (((0,), (0,)), ((), ())), preferred_element_type=jnp.float32
    )
    return (counts.astype(jnp.float32) / approx).astype(jnp.bfloat16)


def per_device(counts, cell_factor, gene_factor):
    factor_now = cell_factor
    gene_now = gene_factor
    for step in range(ITERS):
        cell_copy = factor_now.astype(jnp.bfloat16)
        gene_copy = gene_now.astype(jnp.bfloat16)
        ratio = ratio_tile(counts, cell_copy, gene_copy)
        partial_value = jnp.dot(cell_copy, ratio, preferred_element_type=jnp.float32)
        column_sums = jnp.sum(factor_now, axis=1)
        numerator, denominator = lax.psum((partial_value, column_sums), "cell")
        gene_now = gene_now * numerator / denominator[:, None]
        new_copy = gene_now.astype(jnp.bfloat16)
        ratio = ratio_tile(counts, cell_copy, new_copy)
        cell_partial = lax.dot_general(
            new_copy, ratio, (((1,), (1,)), ((), ())), preferred_element_type=jnp.float32
        )
        gene_sums = jnp.sum(gene_now, axis=1)
        cell_numer, cell_denom = lax.psum((cell_partial, gene_sums), "gene")
        factor_now = factor_now * cell_numer / cell_denom[:, None]
    return (factor_now, gene_now)


def solution(mesh):
    return jax.shard_map(
        per_device,
        mesh=mesh,
        in_specs=(P("cell", "gene"), P(None, "cell"), P(None, "gene")),
        out_specs=(P(None, "cell"), P(None, "gene")),
        check_vma=False,
    )
```

profile of v0, /device:TPU:8, one launch (start us, length us, event | category | flops | bytes accessed | tf_op | source)
XLA Modules:
  0.0 1204.2 jit_solution(11915715744897430383)
XLA Ops:
  7.2 0.0 copy-start
  7.2 0.0 copy-start.1
  7.2 0.0 all-reduce.7.cloned.1.call-start
  7.2 8.2 fusion.27
  15.4 0.0 all-reduce.7.cloned.1.call-update
  15.4 0.0 all-reduce.9.cloned.1.call-start
  15.5 0.0 copy-done
  15.5 0.1 reduce_sum.54
  15.6 68.1 %psum.85 = f32[32]{0:T(128)S(1)} all-reduce(f32[32]{0:T(128)S(1)} %reduce_sum.54), channel_id=1, replica_groups=mesh['cell'=32,'gene'=8] {'cell'}, use_global_device_ids=true, to_apply=%region_2.0 | all-reduce | flops 32 | bytes 256 | tf_op jit(solution)/shard_map/psum | solution.py:25
  83.8 203.3 %all-reduce.7.cloned.1.call-done = f32[32,2048]{1,0:T(8,128)} async-done(((f32[32,2048]{1,0:T(8,128)}), f32[32,2048]{1,0:T(8,128)}) %all-reduce.7.cloned.1.call-update) | async-done | bytes 262160 | tf_op jit(solution)/shard_map/psum | solution.py:25
  287.1 0.0 copy-done.1
  287.1 1.2 fusion.58
  288.3 8.9 fusion.26
  297.1 0.0 all-reduce.9.cloned.1.call-update
  297.1 0.0 all-reduce.11.cloned.1.call-start
  297.2 31.3 %psum.87 = f32[32]{0:T(128)S(1)} all-reduce(f32[32]{0:T(128)S(1)} %get-tuple-element.10), channel_id=1, replica_groups=mesh['cell'=32,'gene'=8] {'gene'}, use_global_device_ids=true, to_apply=%region_5.0 | all-reduce | flops 32 | bytes 256 | tf_op jit(solution)/shard_map/psum | solution.py:33
  328.5 79.3 %all-reduce.9.cloned.1.call-done = f32[32,2048]{1,0:T(8,128)} async-done(((f32[32,2048]{1,0:T(8,128)}), f32[32,2048]{1,0:T(8,128)}) %all-reduce.9.cloned.1.call-update) | async-done | bytes 262160 | tf_op jit(solution)/shard_map/psum | solution.py:33
  407.7 1.2 fusion.57
  408.9 7.9 fusion.12
  416.8 0.0 all-reduce.11.cloned.1.call-update
  416.8 0.0 all-reduce.13.cloned.1.call-start
  416.9 61.9 %psum.89 = f32[32]{0:T(128)S(1)} all-reduce(f32[32]{0:T(128)S(1)} %get-tuple-element.8), channel_id=1, replica_groups=mesh['cell'=32,'gene'=8] {'cell'}, use_global_device_ids=true, to_apply=%region_8.0 | all-reduce | flops 32 | bytes 256 | tf_op jit(solution)/shard_map/psum | solution.py:25
  478.8 202.0 %all-reduce.11.cloned.1.call-done = f32[32,2048]{1,0:T(8,128)} async-done(((f32[32,2048]{1,0:T(8,128)}), f32[32,2048]{1,0:T(8,128)}) %all-reduce.11.cloned.1.call-update) | async-done | bytes 262160 | tf_op jit(solution)/shard_map/psum | solution.py:25
  680.8 1.2 fusion.56
  682.0 8.9 fusion.10
  690.9 0.0 all-reduce.13.cloned.1.call-update
  690.9 0.0 all-reduce.15.cloned.1.call-start
  691.0 31.3 %psum.91 = f32[32]{0:T(128)S(1)} all-reduce(f32[32]{0:T(128)S(1)} %get-tuple-element.6), channel_id=1, replica_groups=mesh['cell'=32,'gene'=8] {'gene'}, use_global_device_ids=true, to_apply=%region_11.0 | all-reduce | flops 32 | bytes 256 | tf_op jit(solution)/shard_map/psum | solution.py:33
  722.2 79.3 %all-reduce.13.cloned.1.call-done = f32[32,2048]{1,0:T(8,128)} async-done(((f32[32,2048]{1,0:T(8,128)}), f32[32,2048]{1,0:T(8,128)}) %all-reduce.13.cloned.1.call-update) | async-done | bytes 262160 | tf_op jit(solution)/shard_map/psum | solution.py:33
  801.5 1.2 fusion.55
  802.6 7.9 fusion.8
  810.5 0.0 all-reduce.15.cloned.1.call-update
  810.5 0.0 all-reduce.17.cloned.1.call-start
  810.6 61.7 %psum.93 = f32[32]{0:T(128)S(1)} all-reduce(f32[32]{0:T(128)S(1)} %get-tuple-element.4), channel_id=1, replica_groups=mesh['cell'=32,'gene'=8] {'cell'}, use_global_device_ids=true, to_apply=%region_14.0 | all-reduce | flops 32 | bytes 256 | tf_op jit(solution)/shard_map/psum | solution.py:25
  872.3 202.2 %all-reduce.15.cloned.1.call-done = f32[32,2048]{1,0:T(8,128)} async-done(((f32[32,2048]{1,0:T(8,128)}), f32[32,2048]{1,0:T(8,128)}) %all-reduce.15.cloned.1.call-update) | async-done | bytes 262160 | tf_op jit(solution)/shard_map/psum | solution.py:25
  1074.6 1.2 fusion.54
  1075.7 0.0 copy-start.2
  1075.7 9.0 fusion.6
  1084.7 0.0 copy-done.2
  1084.7 0.0 all-reduce.17.cloned.1.call-update
  1084.8 31.3 %psum.95 = f32[32]{0:T(128)S(1)} all-reduce(f32[32]{0:T(128)S(1)} %get-tuple-element.2), channel_id=1, replica_groups=mesh['cell'=32,'gene'=8] {'gene'}, use_global_device_ids=true, to_apply=%region_17.0 | all-reduce | flops 32 | bytes 256 | tf_op jit(solution)/shard_map/psum | solution.py:33
  1116.0 79.5 %all-reduce.17.cloned.1.call-done = f32[32,2048]{1,0:T(8,128)} async-done(((f32[32,2048]{1,0:T(8,128)}), f32[32,2048]{1,0:T(8,128)}) %all-reduce.17.cloned.1.call-update) | async-done | bytes 262160 | tf_op jit(solution)/shard_map/psum | solution.py:33
  1195.6 1.7 multiply_divide_fusion
Async XLA Ops:
  7.2 8.3 copy-start
  7.2 279.9 %copy-start.1 = (f32[32,2048]{1,0:T(8,128)S(1)}, f32[32,2048]{1,0:T(8,128)}, u32[]{:S(2)}) copy-start(f32[32,2048]{1,0:T(8,128)} %param.5) | copy-start | bytes 786436
  7.2 279.9 %all-reduce.7.cloned.1.call-start = ((), (), s32[]{:S(2)}) async-start(), calls=%async_computation | async-start | bytes 524288 | tf_op jit(solution)/shard_map/psum | solution.py:25
  15.4 392.3 %all-reduce.9.cloned.1.call-start = ((), (), s32[]{:S(2)}) async-start(), calls=%async_computation.1 | async-start | bytes 524288 | tf_op jit(solution)/shard_map/psum | solution.py:33
  297.1 383.7 %all-reduce.11.cloned.1.call-start = ((), (), s32[]{:S(2)}) async-start(), calls=%async_computation.2 | async-start | bytes 524288 | tf_op jit(solution)/shard_map/psum | solution.py:25
  416.8 384.7 %all-reduce.13.cloned.1.call-start = ((), (), s32[]{:S(2)}) async-start(), calls=%async_computation.3 | async-start | bytes 524288 | tf_op jit(solution)/shard_map/psum | solution.py:33
  690.9 383.7 %all-reduce.15.cloned.1.call-start = ((), (), s32[]{:S(2)}) async-start(), calls=%async_computation.4 | async-start | bytes 524288 | tf_op jit(solution)/shard_map/psum | solution.py:25
  810.5 385.0 %all-reduce.17.cloned.1.call-start = ((), (), s32[]{:S(2)}) async-start(), calls=%async_computation.5 | async-start | bytes 524288 | tf_op jit(solution)/shard_map/psum | solution.py:33
  1075.7 9.0 copy-start.2
Sparse Core Ops, SparseCore 0:
  15.6 271.4 all-reduce.6
  297.3 110.4 all-reduce.8
  416.9 263.8 all-reduce.10
  691.0 110.4 all-reduce.12
  810.7 263.8 all-reduce.14
  1084.9 110.6 all-reduce.16
where the time goes:
time: 1200 us
  waiting for transfers between devices  846 us (70%)
  blocking collectives  286 us (24%)
  matrix products  50.7 us (4%)
  between operations  14.1 us (1%)
    psum x3, waiting for transfers between devices, per_device(): numerator, denominator = lax.psum((partial_value, column_sums), 'cell')  608 us
    psum x3, waiting for transfers between devices, per_device(): cell_numer, cell_denom = lax.psum((cell_partial, gene_sums), 'gene')  238 us
    psum x3, blocking collectives, per_device(): numerator, denominator = lax.psum((partial_value, column_sums), 'cell')  192 us
    psum x3, blocking collectives, per_device(): cell_numer, cell_denom = lax.psum((cell_partial, gene_sums), 'gene')  93.8 us
    dot_general x3, matrix products, per_device(): lax.dot_general(new_copy, ratio, (((1,), (1,)), ((), ())), preferred_elem...  26.8 us
  transfers between devices with their start and end apart: 6, of which 6 were waited for; matrix products, arithmetic and copies ran while one was open for 0% of the time, Pallas kernels for 0%

commit v1 on v0

v1 whole, which is shorter than its diff:
```python
import functools

import jax
import jax.numpy as jnp
from jax import lax
from jax.experimental import pallas as pl
from jax.experimental.pallas import tpu as pltpu
from jax.sharding import Mesh
from jax.sharding import PartitionSpec as P

ITERS = 3
RANK = 32
GROUPS = 4
LANES = 128
TILE, WIDE, HIGH = 256, 1024, 512
CORES, Y, X = 2, 4, 4
SMALL_VMEM, PASS_VMEM = 4 << 20, 28 << 20
F32, BF16 = jnp.float32, jnp.bfloat16

AT_CORE, AT_Y, AT_X = range(3)


def struct(shape, dtype=F32):
    return jax.ShapeDtypeStruct(shape, dtype)


def kernel_call(kernel, info, operands, out_shape, scratch=(), vmem=SMALL_VMEM, cost=None):
    return pl.pallas_call(
        kernel,
        grid_spec=pltpu.PrefetchScalarGridSpec(
            num_scalar_prefetch=1,
            grid=(),
            in_specs=[pl.BlockSpec(memory_space=pltpu.VMEM)] * len(operands),
            out_specs=jax.tree.map(lambda _: pl.BlockSpec(memory_space=pltpu.VMEM), out_shape),
            scratch_shapes=list(scratch),
        ),
        out_shape=out_shape,
        compiler_params=pltpu.CompilerParams(vmem_limit_bytes=vmem),
        cost_estimate=cost,
    )(info, *operands)


def pass_cost(cells, genes):
    return pl.CostEstimate(flops=cells * genes, bytes_accessed=cells * genes // 8, transcendentals=0)


def ratio_of(counts, approx):
    return (counts.astype(F32) * pl.reciprocal(approx, approx=True)).astype(BF16)


def half_of(info, refs, mine):
    if len(refs) == 2:
        return refs[0 if mine else 1]
    half = refs[0].shape[2] // CORES
    side = info[AT_CORE] if mine else 1 - info[AT_CORE]
    return refs[0].at[:, :, pl.ds(pl.multiple_of(side * half, half), half)]


def gene_block(side, counts_ref, cell_copy, cell_turned, sums, groups, out_ref):
    n_cells = counts_ref.shape[0]
    half = out_ref.shape[2] - LANES
    base = side * half

    @pl.loop(0, half // WIDE)
    def _(j):
        at = pl.multiple_of(j * WIDE, WIDE)
        cols = pl.ds(pl.multiple_of(base + at, WIDE), WIDE)
        genes = groups[:, :, pl.ds(at, WIDE)].reshape(RANK, WIDE).astype(BF16)
        numer = jnp.zeros((RANK, WIDE), F32)
        for start in range(0, n_cells, TILE):
            rows = slice(start, start + TILE)
            approx = jnp.dot(cell_turned[rows, :], genes, preferred_element_type=F32)
            ratio = ratio_of(counts_ref[rows, cols], approx)
            numer = numer + jnp.dot(cell_copy[:, rows], ratio, preferred_element_type=F32)
        out_ref[:, :, pl.ds(at, WIDE)] = numer.reshape(GROUPS, 8, WIDE)

    out_ref[:, :, half:] = sums[...].reshape(GROUPS, 8, LANES)


def gene_first_kernel(info, counts_ref, cells_ref, *refs):
    gene_refs, (out_ref, cell_copy, cell_turned, sums) = refs[:-4], refs[-4:]
    cells = cells_ref[...].reshape(RANK, cells_ref.shape[2])
    cell_copy[...] = cells.astype(BF16)
    cell_turned[...] = cells.T.astype(BF16)
    sums[...] = jnp.broadcast_to(jnp.sum(cells, axis=1, keepdims=True), (RANK, LANES))
    gene_block(
        1 - info[AT_CORE], counts_ref, cell_copy, cell_turned, sums, half_of(info, gene_refs, False), out_ref
    )


def gene_second_kernel(info, counts_ref, cell_copy, cell_turned, sums, *refs):
    gene_block(
        info[AT_CORE], counts_ref, cell_copy, cell_turned, sums, half_of(info, refs[:-1], True), refs[-1]
    )


def gene_half(info, counts, left, genes):
    first = len(left) == 1
    n_cells, n_genes = counts.shape
    half = n_genes // CORES
    sums = struct((GROUPS, 8, half + LANES))
    made = [struct((RANK, n_cells), BF16), struct((n_cells, RANK), BF16), struct((RANK, LANES))]
    return kernel_call(
        gene_first_kernel if first else gene_second_kernel,
        info,
        (counts, *left, *genes),
        [sums] + made if first else [sums],
        vmem=PASS_VMEM,
        cost=pass_cost(n_cells, half),
    )


def cell_kernel(info, counts_ref, cells_ref, mine_ref, other_ref, out_ref, ordered, gene_copy):
    n_cells, n_genes = counts_ref.shape
    half = n_genes // CORES
    for side, ref in ((info[AT_CORE], mine_ref), (1 - info[AT_CORE], other_ref)):
        ordered[:, :, pl.ds(pl.multiple_of(side * half, half), half)] = ref[...]
    factor = ordered[...].reshape(RANK, n_genes)
    gene_copy[...] = factor.astype(BF16)
    sums = jnp.broadcast_to(jnp.sum(factor, axis=1, keepdims=True), (RANK, LANES))
    out_ref[:, :, n_cells:] = sums.reshape(GROUPS, 8, LANES)

    @pl.loop(0, n_cells // HIGH)
    def _(i):
        at = pl.multiple_of(i * HIGH, HIGH)
        rows = pl.ds(at, HIGH)
        cells = cells_ref[:, :, rows].reshape(RANK, HIGH).T.astype(BF16)
        numer = jnp.zeros((RANK, HIGH), F32)
        for start in range(0, n_genes, HIGH):
            cols = slice(start, start + HIGH)
            genes = gene_copy[:, cols]
            approx = jnp.dot(cells, genes, preferred_element_type=F32)
            ratio = ratio_of(counts_ref[rows, cols], approx)
            numer = numer + lax.dot_general(genes, ratio, (((1,), (1,)), ((), ())), preferred_element_type=F32)
        out_ref[:, :, rows] = numer.reshape(GROUPS, 8, HIGH)


def cell_pass(info, counts, cells, mine, other):
    n_cells, n_genes = counts.shape
    return kernel_call(
        cell_kernel,
        info,
        (counts, cells, mine, other),
        struct((GROUPS, 8, n_cells + LANES)),
        [pltpu.VMEM((GROUPS, 8, n_genes), F32), pltpu.VMEM((RANK, n_genes), BF16)],
        vmem=PASS_VMEM,
        cost=pass_cost(n_cells, n_genes),
    )


def pair_sum_kernel(info, a_ref, b_ref, out_ref):
    out_ref[...] = a_ref[...] + b_ref[...]


def spread_sum_kernel(info, parts_ref, out_ref):
    total = parts_ref[0]
    for i in range(1, parts_ref.shape[0]):
        total = total + parts_ref[i]
    for i in range(out_ref.shape[0]):
        out_ref[i] = total


def sum_kernel(info, parts_ref, out_ref):
    total = parts_ref[0]
    for i in range(1, parts_ref.shape[0]):
        total = total + parts_ref[i]
    out_ref[...] = total


def put_updated(piece, total, out_ref):
    width = piece.shape[1]
    new = piece * total[:, :width] / total[:, width : width + 1]
    for i in range(out_ref.shape[0]):
        out_ref[i] = new


def gene_update_kernel(info, parts_ref, *refs):
    total = parts_ref[0]
    for i in range(1, parts_ref.shape[0]):
        total = total + parts_ref[i]
    put_updated(half_of(info, refs[:-1], True)[info[AT_Y]], total, refs[-1])


def cell_update_kernel(info, cells_ref, *refs):
    total = refs[0][...]
    for ref in refs[1:-1]:
        total = total + ref[...]
    put_updated(cells_ref[info[AT_X]], total, refs[-1])


def join_genes_kernel(info, mine_ref, other_ref, out_ref):
    half = mine_ref.shape[2]
    for side, ref in ((info[AT_CORE], mine_ref), (1 - info[AT_CORE], other_ref)):
        out_ref[:, :, pl.ds(pl.multiple_of(side * half, half), half)] = ref[...]


def swap(a, axis):
    return lax.all_to_all(a, axis, 0, 0, tiled=True)


def per_device(n_z, n_zhi, counts, cell_factor, gene_factor):
    n_cells, n_genes = counts.shape
    half = n_genes // CORES
    info = jnp.stack([lax.axis_index(a) for a in ("core", "y", "x")]).astype(jnp.int32)
    to_core = lambda a: lax.ppermute(a, "core", [(0, 1), (1, 0)])
    to_zhi = lambda a, s: lax.ppermute(a, "z_hi", [(i, (i + s) % n_zhi) for i in range(n_zhi)])

    cells = cell_factor.reshape(GROUPS, 8, n_cells)
    genes = [gene_factor.reshape(GROUPS, 8, n_genes)]
    wide, long = half + LANES, n_cells + LANES
    for step in range(ITERS):
        sent, *left = gene_half(info, counts, [cells], genes)
        got = to_core(sent)
        kept = gene_half(info, counts, left, genes)[0]
        both = kernel_call(pair_sum_kernel, info, (kept, got), struct((Y, 8, wide)))
        part = kernel_call(spread_sum_kernel, info, (swap(both, "y"),), struct((n_z, 8, wide)))
        mine = kernel_call(gene_update_kernel, info, (swap(part, "z"), *genes), struct((Y, 8, half)))
        mine = swap(mine, "y")
        genes = [mine, to_core(mine)]

        sums = cell_pass(info, counts, cells, *genes)
        part = kernel_call(sum_kernel, info, (swap(sums, "x"),), struct((8, long)))
        got = [to_zhi(part, s) for s in range(1, n_zhi)]
        cells = kernel_call(cell_update_kernel, info, (cells, part, *got), struct((X, 8, n_cells)))
        cells = swap(cells, "x")
    joined = kernel_call(join_genes_kernel, info, genes, struct((GROUPS, 8, n_genes)))
    return cells.reshape(RANK, n_cells), joined.reshape(RANK, n_genes)


def solution(mesh):
    n_z, n_zhi = mesh.shape["cell"] // (Y * CORES), mesh.shape["gene"] // X
    cut = Mesh(mesh.devices.reshape(n_z, Y, CORES, n_zhi, X), ("z", "y", "core", "z_hi", "x"))
    cell, gene = ("z", "y", "core"), ("z_hi", "x")
    return jax.shard_map(
        functools.partial(per_device, n_z, n_zhi),
        mesh=cut,
        in_specs=(P(cell, gene), P(None, cell), P(None, gene)),
        out_specs=(P(None, cell), P(None, gene)),
        check_vma=False,
    )
```

time: 1200 us -> 227 us (0.19)
  waiting for transfers between devices: 846 us -> 23.1 us
  blocking collectives: 286 us -> 131 us
  matrix products: 50.7 us -> 0 us
  Pallas kernels: 0 us -> 47.7 us
  starting transfers between devices: 0.25 us -> 16.9 us
  between operations: 14.1 us -> 0.81 us
    psum x6 -> x0, waiting for transfers between devices: 846 us -> none  [the longest x3 608 us: per_device(): numerator, denominator = lax.psum((partial_value, column_sums), 'cell')]
    psum x6 -> x0, blocking collectives: 286 us -> none  [the longest x3 192 us: per_device(): numerator, denominator = lax.psum((partial_value, column_sums), 'cell')]
    all_to_all x0 -> x14, blocking collectives: none -> 131 us  [swap(): return lax.all_to_all(a, axis, 0, 0, tiled=True)]
    dot_general x6 -> x0, matrix products: 50.7 us -> none  [the longest x3 26.8 us: per_device(): lax.dot_general(new_copy, ratio, (((1,), (1,)), ((), ())), preferred_elem...]
    pallas_call x0 -> x25, Pallas kernels: none -> 47.7 us  [kernel_call(): pl.pallas_call(kernel, grid_spec=pltpu.PrefetchScalarGridSpec(num_scalar_...]
    ppermute x0 -> x9, waiting for transfers between devices: none -> 17.7 us  [the longest x3 13.6 us: per_device(): lax.ppermute(a, 'z_hi', [(i, (i + s) % n_zhi) for i in range(n_zhi)])]
    ppermute x0 -> x9, starting transfers between devices: none -> 13.5 us  [the longest x3 13.4 us: per_device(): lax.ppermute(a, 'z_hi', [(i, (i + s) % n_zhi) for i in range(n_zhi)])]
  transfers between devices with their start and end apart: 6 -> 10, of which waited for: 6 -> 7; matrix products, arithmetic and copies ran while one was open for 0% -> 0% of each run, Pallas kernels for 0% -> 4%
where the time goes in v1:
time: 227 us; the launch traced here: 226 us
  blocking collectives  131 us (58%)
  Pallas kernels  47.7 us (21%)
  waiting for transfers between devices  23.1 us (10%)
  starting transfers between devices  16.9 us (7%)
  local copies, waits for them, and re-layouts  5.99 us (3%)
    all_to_all x14, blocking collectives, swap(): return lax.all_to_all(a, axis, 0, 0, tiled=True)  131 us
    pallas_call x25, Pallas kernels, kernel_call(): pl.pallas_call(kernel, grid_spec=pltpu.PrefetchScalarGridSpec(num_scalar_...  47.7 us
    ppermute x3, waiting for transfers between devices, per_device(): lax.ppermute(a, 'z_hi', [(i, (i + s) % n_zhi) for i in range(n_zhi)])  13.6 us
    ppermute x3, starting transfers between devices, per_device(): lax.ppermute(a, 'z_hi', [(i, (i + s) % n_zhi) for i in range(n_zhi)])  13.4 us
    unnamed x9, local copies, waits for them, and re-layouts  5.99 us
    all_to_all x1, waiting for transfers between devices, swap(): return lax.all_to_all(a, axis, 0, 0, tiled=True)  5.38 us
  transfers between devices with their start and end apart: 10, of which 7 were waited for; matrix products, arithmetic and copies ran while one was open for 0% of the time, Pallas kernels for 4%

profile of v1, /device:TPU:8, one launch (start us, length us, event | category | flops | bytes accessed | tf_op | source)
XLA Modules:
  0.0 225.8 jit_solution(8948080435344020231)
XLA Ops:
  0.6 0.1 pad_add_fusion.info
  0.7 3.4 %copy-done = bf16[2048,2048]{1,0:T(8,128)(2,1)S(1)} copy-done((bf16[2048,2048]{1,0:T(8,128)(2,1)S(1)}, bf16[2048,2048]{1,0:T(8,128)(2,1)}, u32[]{:S(2)}) %copy-start) | copy-done | bytes 8388632
  4.1 0.9 copy-done.1
  5.0 0.9 copy-done.3
  6.0 3.1 %shard_map.50 = (f32[4,8,1152]{2,1,0:T(8,128)S(1)}, bf16[32,2048]{1,0:T(8,128)(2,1)S(1)}, bf16[2048,32]{1,0:T(8,128)(2,1)S(1)}, f32[32,128]{1,0:T(8,128)S(1)}) custom-call(s32[3]{0:T(128)S(1)} %pad_add_fusion.info, bf16[2048,2048]{1,0:T(8,128)(2,1)S(1)} %copy-done, f32[4,8,2048]{2,1,0:T(8,128)S(1)} %bitcast.10, f32[4,8,2048]{2,1,0:T(8,128)S(1)} %bitcast.7), custom_call_target="tpu_custom_call" | custom-call | flops 2097152 | bytes 262144 | tf_op jit(solution)/shard_map/pallas_call | solution.py:28
  9.1 0.0 collective-permute-start
  9.1 3.0 %shard_map.51.a_ref = f32[4,8,1152]{2,1,0:T(8,128)S(1)} custom-call(s32[3]{0:T(128)S(1)} %pad_add_fusion.info, bf16[2048,2048]{1,0:T(8,128)(2,1)S(1)} %copy-done, bf16[32,2048]{1,0:T(8,128)(2,1)S(1)} %get-tuple-element.14.cell_copy, bf16[2048,32]{1,0:T(8,128)(2,1)S(1)} %get-tuple-element.15.cell_turned, f32[32,128]{1,0:T(8,128)S(1)} %get-tuple-element.16.sums, ...), custom_call_target="tpu_custom_call" | custom-call | flops 2097152 | bytes 262144 | tf_op jit(solution)/shard_map/pallas_call | solution.py:28
  12.1 0.0 collective-permute-done.b_ref
  12.1 0.6 shard_map.52
  12.6 9.4 %all_to_all.75.parts_ref = f32[4,8,1152]{2,1,0:T(8,128)S(1)} all-to-all(f32[4,8,1152]{2,1,0:T(8,128)S(1)} %shard_map.52), channel_id=1, replica_groups=mesh['z'=4,'y'=4,'core'=2,'z_hi'=2,'x'=4] {'y'}, dimensions={0} | all-to-all | bytes 294912 | tf_op jit(solution)/shard_map/all_to_all | solution.py:198
  22.1 0.6 shard_map.53
  22.6 12.3 %all_to_all.76.parts_ref = f32[4,8,1152]{2,1,0:T(8,128)S(1)} all-to-all(f32[4,8,1152]{2,1,0:T(8,128)S(1)} %shard_map.53), channel_id=1, replica_groups=mesh['z'=4,'y'=4,'core'=2,'z_hi'=2,'x'=4] {'z'}, dimensions={0} | all-to-all | bytes 294912 | tf_op jit(solution)/shard_map/all_to_all | solution.py:198
  34.9 0.6 shard_map.54
  35.5 8.4 %all_to_all.77.mine_ref.refs_0_ = f32[4,8,1024]{2,1,0:T(8,128)S(1)} all-to-all(f32[4,8,1024]{2,1,0:T(8,128)S(1)} %shard_map.54), channel_id=1, replica_groups=mesh['z'=4,'y'=4,'core'=2,'z_hi'=2,'x'=4] {'y'}, dimensions={0} | all-to-all | bytes 262144 | tf_op jit(solution)/shard_map/all_to_all | solution.py:198
  43.9 0.0 collective-permute-start.1
  43.9 1.3 collective-permute-done.1.other_ref.refs_1_
  45.2 6.3 %shard_map.55 = f32[4,8,2176]{2,1,0:T(8,128)S(1)} custom-call(s32[3]{0:T(128)S(1)} %pad_add_fusion.info, bf16[2048,2048]{1,0:T(8,128)(2,1)S(1)} %copy-done, f32[4,8,2048]{2,1,0:T(8,128)S(1)} %bitcast.11, f32[4,8,1024]{2,1,0:T(8,128)S(1)} %all_to_all.77.mine_ref.refs_0_, f32[4,8,1024]{2,1,0:T(8,128)S(1)} %collective-permute-done.1.other_ref.refs_1_), custom_call_target="tpu_custom_call" | custom-call | flops 4194304 | bytes 524288 | tf_op jit(solution)/shard_map/pallas_call | solution.py:28
  51.6 11.2 %all_to_all.78.parts_ref = f32[4,8,2176]{2,1,0:T(8,128)S(1)} all-to-all(f32[4,8,2176]{2,1,0:T(8,128)S(1)} %shard_map.55), channel_id=1, replica_groups=mesh['z'=4,'y'=4,'core'=2,'z_hi'=2,'x'=4] {'x'}, dimensions={0} | all-to-all | bytes 557056 | tf_op jit(solution)/shard_map/all_to_all | solution.py:198
  62.8 0.6 shard_map.56.refs_0_
  63.4 4.6 %collective-permute-start.2 = (f32[8,2176]{1,0:T(8,128)S(1)}, f32[8,2176]{1,0:T(8,128)S(1)}, u32[]{:S(2)}, u32[]{:S(2)}) collective-permute-start(f32[8,2176]{1,0:T(8,128)S(1)} %shard_map.56.refs_0_), channel_id=1, source_target_pairs={{0,4},{4,0},{1,5},{5,1},{2,6},{6,2},{3,7},{7,3},{8,12},{12,8},{9,1... | collective-permute-start | bytes 208904 | tf_op jit(solution)/shard_map/ppermute | solution.py:206
  68.0 4.3 %collective-permute-done.2.refs_1_ = f32[8,2176]{1,0:T(8,128)S(1)} collective-permute-done((f32[8,2176]{1,0:T(8,128)S(1)}, f32[8,2176]{1,0:T(8,128)S(1)}, u32[]{:S(2)}, u32[]{:S(2)}) %collective-permute-start.2) | collective-permute-done | bytes 69664 | tf_op jit(solution)/shard_map/ppermute | solution.py:206
  72.3 0.6 shard_map.57
  72.9 9.1 %all_to_all.79.cells_ref = f32[4,8,2048]{2,1,0:T(8,128)S(1)} all-to-all(f32[4,8,2048]{2,1,0:T(8,128)S(1)} %shard_map.57), channel_id=1, replica_groups=mesh['z'=4,'y'=4,'core'=2,'z_hi'=2,'x'=4] {'x'}, dimensions={0} | all-to-all | bytes 524288 | tf_op jit(solution)/shard_map/all_to_all | solution.py:198
  82.0 3.1 %shard_map.58 = (f32[4,8,1152]{2,1,0:T(8,128)S(1)}, bf16[32,2048]{1,0:T(8,128)(2,1)S(1)}, bf16[2048,32]{1,0:T(8,128)(2,1)S(1)}, f32[32,128]{1,0:T(8,128)S(1)}) custom-call(s32[3]{0:T(128)S(1)} %pad_add_fusion.info, bf16[2048,2048]{1,0:T(8,128)(2,1)S(1)} %copy-done, f32[4,8,2048]{2,1,0:T(8,128)S(1)} %all_to_all.79.cells_ref, ...), custom_call_target="tpu_custom_call" | custom-call | flops 2097152 | bytes 262144 | tf_op jit(solution)/shard_map/pallas_call | solution.py:28
  85.0 0.0 collective-permute-start.3
  85.1 2.9 %shard_map.59.a_ref = f32[4,8,1152]{2,1,0:T(8,128)S(1)} custom-call(s32[3]{0:T(128)S(1)} %pad_add_fusion.info, bf16[2048,2048]{1,0:T(8,128)(2,1)S(1)} %copy-done, bf16[32,2048]{1,0:T(8,128)(2,1)S(1)} %get-tuple-element.18.cell_copy, bf16[2048,32]{1,0:T(8,128)(2,1)S(1)} %get-tuple-element.19.cell_turned, f32[32,128]{1,0:T(8,128)S(1)} %get-tuple-element.20.sums, ...), custom_call_target="tpu_custom_call" | custom-call | flops 2097152 | bytes 262144 | tf_op jit(solution)/shard_map/pallas_call | solution.py:28
  88.0 0.0 collective-permute-done.3.b_ref
  88.0 0.6 shard_map.60
  88.6 8.7 %all_to_all.80.parts_ref = f32[4,8,1152]{2,1,0:T(8,128)S(1)} all-to-all(f32[4,8,1152]{2,1,0:T(8,128)S(1)} %shard_map.60), channel_id=1, replica_groups=mesh['z'=4,'y'=4,'core'=2,'z_hi'=2,'x'=4] {'y'}, dimensions={0} | all-to-all | bytes 294912 | tf_op jit(solution)/shard_map/all_to_all | solution.py:198
  97.3 0.6 shard_map.61
  97.9 9.0 %all_to_all.81.parts_ref = f32[4,8,1152]{2,1,0:T(8,128)S(1)} all-to-all(f32[4,8,1152]{2,1,0:T(8,128)S(1)} %shard_map.61), channel_id=1, replica_groups=mesh['z'=4,'y'=4,'core'=2,'z_hi'=2,'x'=4] {'z'}, dimensions={0} | all-to-all | bytes 294912 | tf_op jit(solution)/shard_map/all_to_all | solution.py:198
  106.9 0.6 shard_map.62
  107.5 8.4 %all_to_all.82.mine_ref.refs_0_ = f32[4,8,1024]{2,1,0:T(8,128)S(1)} all-to-all(f32[4,8,1024]{2,1,0:T(8,128)S(1)} %shard_map.62), channel_id=1, replica_groups=mesh['z'=4,'y'=4,'core'=2,'z_hi'=2,'x'=4] {'y'}, dimensions={0} | all-to-all | bytes 262144 | tf_op jit(solution)/shard_map/all_to_all | solution.py:198
  115.9 0.0 collective-permute-start.4
  115.9 1.3 collective-permute-done.4.other_ref.refs_1_
  117.3 6.3 %shard_map.63 = f32[4,8,2176]{2,1,0:T(8,128)S(1)} custom-call(s32[3]{0:T(128)S(1)} %pad_add_fusion.info, bf16[2048,2048]{1,0:T(8,128)(2,1)S(1)} %copy-done, f32[4,8,2048]{2,1,0:T(8,128)S(1)} %all_to_all.79.cells_ref, f32[4,8,1024]{2,1,0:T(8,128)S(1)} %all_to_all.82.mine_ref.refs_0_, f32[4,8,1024]{2,1,0:T(8,128)S(1)} %collective-permute-done.4.other_ref.refs_1_), custom_call_target="tpu_custom_call" | custom-call | flops 4194304 | bytes 524288 | tf_op jit(solution)/shard_map/pallas_call | solution.py:28
  123.6 9.8 %all_to_all.83.parts_ref = f32[4,8,2176]{2,1,0:T(8,128)S(1)} all-to-all(f32[4,8,2176]{2,1,0:T(8,128)S(1)} %shard_map.63), channel_id=1, replica_groups=mesh['z'=4,'y'=4,'core'=2,'z_hi'=2,'x'=4] {'x'}, dimensions={0} | all-to-all | bytes 557056 | tf_op jit(solution)/shard_map/all_to_all | solution.py:198
  133.4 0.6 shard_map.64.refs_0_
  133.9 4.4 %collective-permute-start.5 = (f32[8,2176]{1,0:T(8,128)S(1)}, f32[8,2176]{1,0:T(8,128)S(1)}, u32[]{:S(2)}, u32[]{:S(2)}) collective-permute-start(f32[8,2176]{1,0:T(8,128)S(1)} %shard_map.64.refs_0_), channel_id=1, source_target_pairs={{0,4},{4,0},{1,5},{5,1},{2,6},{6,2},{3,7},{7,3},{8,12},{12,8},{9,1... | collective-permute-start | bytes 208904 | tf_op jit(solution)/shard_map/ppermute | solution.py:206
  138.3 4.7 %collective-permute-done.5.refs_1_ = f32[8,2176]{1,0:T(8,128)S(1)} collective-permute-done((f32[8,2176]{1,0:T(8,128)S(1)}, f32[8,2176]{1,0:T(8,128)S(1)}, u32[]{:S(2)}, u32[]{:S(2)}) %collective-permute-start.5) | collective-permute-done | bytes 69664 | tf_op jit(solution)/shard_map/ppermute | solution.py:206
  143.0 0.6 shard_map.65
  143.6 9.1 %all_to_all.84.cells_ref = f32[4,8,2048]{2,1,0:T(8,128)S(1)} all-to-all(f32[4,8,2048]{2,1,0:T(8,128)S(1)} %shard_map.65), channel_id=1, replica_groups=mesh['z'=4,'y'=4,'core'=2,'z_hi'=2,'x'=4] {'x'}, dimensions={0} | all-to-all | bytes 524288 | tf_op jit(solution)/shard_map/all_to_all | solution.py:198
  152.7 3.1 %shard_map.66 = (f32[4,8,1152]{2,1,0:T(8,128)S(1)}, bf16[32,2048]{1,0:T(8,128)(2,1)S(1)}, bf16[2048,32]{1,0:T(8,128)(2,1)S(1)}, f32[32,128]{1,0:T(8,128)S(1)}) custom-call(s32[3]{0:T(128)S(1)} %pad_add_fusion.info, bf16[2048,2048]{1,0:T(8,128)(2,1)S(1)} %copy-done, f32[4,8,2048]{2,1,0:T(8,128)S(1)} %all_to_all.84.cells_ref, ...), custom_call_target="tpu_custom_call" | custom-call | flops 2097152 | bytes 262144 | tf_op jit(solution)/shard_map/pallas_call | solution.py:28
  155.7 0.0 collective-permute-start.6
  155.8 2.9 %shard_map.67.a_ref = f32[4,8,1152]{2,1,0:T(8,128)S(1)} custom-call(s32[3]{0:T(128)S(1)} %pad_add_fusion.info, bf16[2048,2048]{1,0:T(8,128)(2,1)S(1)} %copy-done, bf16[32,2048]{1,0:T(8,128)(2,1)S(1)} %get-tuple-element.22.cell_copy, bf16[2048,32]{1,0:T(8,128)(2,1)S(1)} %get-tuple-element.23.cell_turned, f32[32,128]{1,0:T(8,128)S(1)} %get-tuple-element.24.sums, ...), custom_call_target="tpu_custom_call" | custom-call | flops 2097152 | bytes 262144 | tf_op jit(solution)/shard_map/pallas_call | solution.py:28
  158.7 0.0 collective-permute-done.6.b_ref
  158.7 0.6 shard_map.68
  159.3 8.7 %all_to_all.85.parts_ref = f32[4,8,1152]{2,1,0:T(8,128)S(1)} all-to-all(f32[4,8,1152]{2,1,0:T(8,128)S(1)} %shard_map.68), channel_id=1, replica_groups=mesh['z'=4,'y'=4,'core'=2,'z_hi'=2,'x'=4] {'y'}, dimensions={0} | all-to-all | bytes 294912 | tf_op jit(solution)/shard_map/all_to_all | solution.py:198
  168.0 0.6 shard_map.69
  168.6 9.0 %all_to_all.86.parts_ref = f32[4,8,1152]{2,1,0:T(8,128)S(1)} all-to-all(f32[4,8,1152]{2,1,0:T(8,128)S(1)} %shard_map.69), channel_id=1, replica_groups=mesh['z'=4,'y'=4,'core'=2,'z_hi'=2,'x'=4] {'z'}, dimensions={0} | all-to-all | bytes 294912 | tf_op jit(solution)/shard_map/all_to_all | solution.py:198
  177.6 0.6 shard_map.70
  178.2 8.4 %all_to_all.87.mine_ref = f32[4,8,1024]{2,1,0:T(8,128)S(1)} all-to-all(f32[4,8,1024]{2,1,0:T(8,128)S(1)} %shard_map.70), channel_id=1, replica_groups=mesh['z'=4,'y'=4,'core'=2,'z_hi'=2,'x'=4] {'y'}, dimensions={0} | all-to-all | bytes 262144 | tf_op jit(solution)/shard_map/all_to_all | solution.py:198
  186.6 0.0 collective-permute-start.7
  186.6 1.3 collective-permute-done.7.other_ref
  187.9 6.3 %shard_map.71 = f32[4,8,2176]{2,1,0:T(8,128)S(1)} custom-call(s32[3]{0:T(128)S(1)} %pad_add_fusion.info, bf16[2048,2048]{1,0:T(8,128)(2,1)S(1)} %copy-done, f32[4,8,2048]{2,1,0:T(8,128)S(1)} %all_to_all.84.cells_ref, f32[4,8,1024]{2,1,0:T(8,128)S(1)} %all_to_all.87.mine_ref, f32[4,8,1024]{2,1,0:T(8,128)S(1)} %collective-permute-done.7.other_ref), custom_call_target="tpu_custom_call" | custom-call | flops 4194304 | bytes 524288 | tf_op jit(solution)/shard_map/pallas_call | solution.py:28
  194.2 9.8 %all_to_all.88.parts_ref = f32[4,8,2176]{2,1,0:T(8,128)S(1)} all-to-all(f32[4,8,2176]{2,1,0:T(8,128)S(1)} %shard_map.71), channel_id=1, replica_groups=mesh['z'=4,'y'=4,'core'=2,'z_hi'=2,'x'=4] {'x'}, dimensions={0} | all-to-all | bytes 557056 | tf_op jit(solution)/shard_map/all_to_all | solution.py:198
  204.0 0.6 shard_map.72.refs_0_
  204.6 4.4 %collective-permute-start.8 = (f32[8,2176]{1,0:T(8,128)S(1)}, f32[8,2176]{1,0:T(8,128)S(1)}, u32[]{:S(2)}, u32[]{:S(2)}) collective-permute-start(f32[8,2176]{1,0:T(8,128)S(1)} %shard_map.72.refs_0_), channel_id=1, source_target_pairs={{0,4},{4,0},{1,5},{5,1},{2,6},{6,2},{3,7},{7,3},{8,12},{12,8},{9,1... | collective-permute-start | bytes 208904 | tf_op jit(solution)/shard_map/ppermute | solution.py:206
  209.0 4.6 %collective-permute-done.8.refs_1_ = f32[8,2176]{1,0:T(8,128)S(1)} collective-permute-done((f32[8,2176]{1,0:T(8,128)S(1)}, f32[8,2176]{1,0:T(8,128)S(1)}, u32[]{:S(2)}, u32[]{:S(2)}) %collective-permute-start.8) | collective-permute-done | bytes 69664 | tf_op jit(solution)/shard_map/ppermute | solution.py:206
  213.7 1.3 shard_map.73
  215.0 3.4 %all-to-all-start.14 = ((f32[4,8,2048]{2,1,0:T(8,128)}), f32[4,8,2048]{2,1,0:T(8,128)S(1)}, u32[]{:S(2)}, u32[]{:S(2)}) async-start(f32[4,8,2048]{2,1,0:T(8,128)} %shard_map.73), calls=%async_computation.14 | async-start | bytes 524288 | tf_op jit(solution)/shard_map/all_to_all | solution.py:198
  218.4 1.3 shard_map.74
  219.7 5.4 %all-to-all-done.14 = f32[4,8,2048]{2,1,0:T(8,128)S(1)} async-done(((f32[4,8,2048]{2,1,0:T(8,128)}), f32[4,8,2048]{2,1,0:T(8,128)S(1)}, u32[]{:S(2)}, u32[]{:S(2)}) %all-to-all-start.14) | async-done | bytes 262176 | tf_op jit(solution)/shard_map/all_to_all | solution.py:198
  225.0 0.7 copy.6
  (5 shorter events, 0.0 us)
Async XLA Ops:
  0.7 3.4 %copy-start = (bf16[2048,2048]{1,0:T(8,128)(2,1)S(1)}, bf16[2048,2048]{1,0:T(8,128)(2,1)}, u32[]{:S(2)}) copy-start(bf16[2048,2048]{1,0:T(8,128)(2,1)} %counts_ref.17) | copy-start | bytes 25165828
  4.1 0.9 copy-start.1
  5.0 0.9 copy-start.3
  6.0 3.1 %copy-start.2 = (f32[32,2048]{1,0:T(8,128)S(1)}, f32[32,2048]{1,0:T(8,128)}, u32[]{:S(2)}) copy-start(f32[32,2048]{1,0:T(8,128)} %param.5) | copy-start | bytes 786436
  9.1 3.0 %collective-permute-start = (f32[4,8,1152]{2,1,0:T(8,128)S(1)}, f32[4,8,1152]{2,1,0:T(8,128)S(1)}, u32[]{:S(2)}, u32[]{:S(2)}) collective-permute-start(f32[4,8,1152]{2,1,0:T(8,128)S(1)} %get-tuple-element.17), channel_id=1, source_target_pairs={{0,8},{8,0},{1,9},{9,1},{2,10},{10,2},{3,11},{11,3},{4,12},{12,4},... | collective-permute-start | bytes 442376 | tf_op jit(solution)/shard_map/ppermute | solution.py:205
  43.9 1.3 collective-permute-start.1
  63.4 8.9 %collective-permute-start.2 = (f32[8,2176]{1,0:T(8,128)S(1)}, f32[8,2176]{1,0:T(8,128)S(1)}, u32[]{:S(2)}, u32[]{:S(2)}) collective-permute-start(f32[8,2176]{1,0:T(8,128)S(1)} %shard_map.56.refs_0_), channel_id=1, source_target_pairs={{0,4},{4,0},{1,5},{5,1},{2,6},{6,2},{3,7},{7,3},{8,12},{12,8},{9,1... | collective-permute-start | bytes 208904 | tf_op jit(solution)/shard_map/ppermute | solution.py:206
  85.0 3.0 %collective-permute-start.3 = (f32[4,8,1152]{2,1,0:T(8,128)S(1)}, f32[4,8,1152]{2,1,0:T(8,128)S(1)}, u32[]{:S(2)}, u32[]{:S(2)}) collective-permute-start(f32[4,8,1152]{2,1,0:T(8,128)S(1)} %get-tuple-element.21), channel_id=1, source_target_pairs={{0,8},{8,0},{1,9},{9,1},{2,10},{10,2},{3,11},{11,3},{4,12},{12,4},... | collective-permute-start | bytes 442376 | tf_op jit(solution)/shard_map/ppermute | solution.py:205
  115.9 1.3 collective-permute-start.4
  133.9 9.1 %collective-permute-start.5 = (f32[8,2176]{1,0:T(8,128)S(1)}, f32[8,2176]{1,0:T(8,128)S(1)}, u32[]{:S(2)}, u32[]{:S(2)}) collective-permute-start(f32[8,2176]{1,0:T(8,128)S(1)} %shard_map.64.refs_0_), channel_id=1, source_target_pairs={{0,4},{4,0},{1,5},{5,1},{2,6},{6,2},{3,7},{7,3},{8,12},{12,8},{9,1... | collective-permute-start | bytes 208904 | tf_op jit(solution)/shard_map/ppermute | solution.py:206
  155.7 3.0 %collective-permute-start.6 = (f32[4,8,1152]{2,1,0:T(8,128)S(1)}, f32[4,8,1152]{2,1,0:T(8,128)S(1)}, u32[]{:S(2)}, u32[]{:S(2)}) collective-permute-start(f32[4,8,1152]{2,1,0:T(8,128)S(1)} %get-tuple-element.25), channel_id=1, source_target_pairs={{0,8},{8,0},{1,9},{9,1},{2,10},{10,2},{3,11},{11,3},{4,12},{12,4},... | collective-permute-start | bytes 442376 | tf_op jit(solution)/shard_map/ppermute | solution.py:205
  186.6 1.3 collective-permute-start.7
  204.6 9.1 %collective-permute-start.8 = (f32[8,2176]{1,0:T(8,128)S(1)}, f32[8,2176]{1,0:T(8,128)S(1)}, u32[]{:S(2)}, u32[]{:S(2)}) collective-permute-start(f32[8,2176]{1,0:T(8,128)S(1)} %shard_map.72.refs_0_), channel_id=1, source_target_pairs={{0,4},{4,0},{1,5},{5,1},{2,6},{6,2},{3,7},{7,3},{8,12},{12,8},{9,1... | collective-permute-start | bytes 208904 | tf_op jit(solution)/shard_map/ppermute | solution.py:206
  215.0 10.1 %all-to-all-start.14 = ((f32[4,8,2048]{2,1,0:T(8,128)}), f32[4,8,2048]{2,1,0:T(8,128)S(1)}, u32[]{:S(2)}, u32[]{:S(2)}) async-start(f32[4,8,2048]{2,1,0:T(8,128)} %shard_map.73), calls=%async_computation.14 | async-start | bytes 524288 | tf_op jit(solution)/shard_map/all_to_all | solution.py:198
